TPU v7x, 32 devices: a whole 2x2x4 slice. The times are simulated.
32 devices in a mesh: node: 16 (over z, y, x), local: 2 (over core).
Axes of the slice: x: 2, y: 2, z: 4, core: 2. Of those that a mesh axis runs over, the one named last changes fastest.
Arguments:
- tokens: bfloat16 [4096, 8192], P(('node', 'local')), may hold values from -6 to 6
- norm_gain: bfloat16 [8192], replicated, may hold values from 0.099609375 to 1.8984375
- key_weight: bfloat16 [8192, 128], P(('node', 'local')), may hold values from -0.0625 to 0.0625
- key_cotangent: bfloat16 [4096, 128], P(('node', 'local')), may hold values from -6 to 6
Outputs:
- keys: bfloat16 [4096, 128], P(('node', 'local'))
- token_grad: bfloat16 [4096, 8192], P(('node', 'local'))
- weight_grad: float32 [8192, 128], P(('node', 'local'))
- gain_grad: float32 [8192], replicated
All inputs are finite; a program needn't handle non-finite values.
Results may differ from a plain program's by a relative error of at most 0.005.
Values may be sent and summed in bfloat16 or wider, within the bound.
A program may use at most 64 MiB of HBM per device.

v0:
```python
import math

import jax
import jax.numpy as jnp
from jax import lax
from jax.sharding import PartitionSpec as P


def local(tokens, norm_gain, key_weight, key_cotangent):
    nodes = lax.axis_size("node")
    locals_count = lax.axis_size("local")
    rows_dev = key_weight.shape[0]
    width = tokens.shape[1]
    tok_rows = tokens.shape[0]
    scale = 1.0 / math.sqrt(tok_rows * nodes * locals_count)
    gain_wide = norm_gain.astype(jnp.float32)
    wide = tokens.astype(jnp.float32)
    rstd = lax.rsqrt(jnp.mean(wide * wide, axis=1, keepdims=True) + 1e-05)
    normed = wide * rstd
    hidden = (normed * gain_wide).astype(jnp.bfloat16)
    secondary = lax.all_gather(key_weight, "node", axis=0, tiled=True)
    permuted = (
        hidden.reshape(tok_rows, nodes, locals_count, rows_dev)
        .transpose(0, 2, 1, 3)
        .reshape(tok_rows, width)
    )
    whole = lax.all_gather(secondary, "local", axis=0, tiled=True)
    keys_wide = jnp.dot(permuted, whole, preferred_element_type=jnp.float32)
    dpermuted = lax.dot_general(
        key_cotangent, whole, (((1,), (1,)), ((), ())), preferred_element_type=jnp.float32
    )
    keys = keys_wide.astype(jnp.bfloat16)
    dhidden = (
        dpermuted.reshape(tok_rows, locals_count, nodes, rows_dev)
        .transpose(0, 2, 1, 3)
        .reshape(tok_rows, width)
    )
    dnormed = dhidden * gain_wide
    inner = jnp.mean(dnormed * normed, axis=1, keepdims=True)
    token_grad = (rstd * (dnormed - normed * inner)).astype(jnp.bfloat16)
    gain_terms = jnp.sum(dhidden * normed, axis=0) * scale
    gain_grad = lax.psum(gain_terms, ("node", "local"))
    partial_grad = lax.psum_scatter(
        lax.dot_general(
            permuted, key_cotangent, (((0,), (0,)), ((), ())), preferred_element_type=jnp.float32
        )
        * scale,
        "local",
        scatter_dimension=0,
        tiled=True,
    )
    weight_grad = lax.psum_scatter(partial_grad, "node", scatter_dimension=0, tiled=True)
    return (keys, token_grad, weight_grad, gain_grad)


def solution(mesh):
    placed = (
        P(("node", "local"), None),
        P(),
        P(("node", "local"), None),
        P(("node", "local"), None),
    )
    return jax.shard_map(
        local,
        mesh=mesh,
        in_specs=placed,
        out_specs=(
            P(("node", "local"), None),
            P(("node", "local"), None),
            P(("node", "local"), None),
            P(),
        ),
        check_vma=False,
    )
```

profile of v0, /device:TPU:0, one launch (start us, length us, event | category | flops | bytes accessed | tf_op | source)
XLA Modules:
  0.0 206.6 jit_solution(14014878901533805670)
XLA Ops:
  7.2 0.0 copy-start
  7.2 0.0 copy-start.2
  7.2 0.0 all-gather.3.cloned.1.call-start
  7.2 0.7 all-gather.3.cloned.1.call-update
  7.9 0.0 all-gather.5.cloned.1.call-start
  8.0 60.8 %all-gather.3.cloned.1.call-done = bf16[4096,128]{1,0:T(8,128)(2,1)} async-done(((bf16[256,128]{1,0:T(8,128)(2,1)}), bf16[4096,128]{1,0:T(8,128)(2,1)}) %all-gather.3.cloned.1.call-update) | async-done | bytes 1048592 | tf_op jit(solution)/shard_map/all_gather | solution.py:21
  68.8 0.0 all-gather.5.cloned.1.call-update
  68.8 0.0 reduce-scatter.3.cloned.1.call-start
  68.9 3.2 %copy.10 = bf16[128,8192]{0,1:T(8,128)(2,1)S(1)} copy(bf16[128,8192]{1,0:T(8,128)(2,1)} %param.4) | data formatting | bytes 4194304 | tf_op args[0]
  72.1 0.0 copy-done.2
  72.1 1.1 fusion.10
  73.2 6.5 %all-gather.5.cloned.1.call-done = bf16[8192,128]{1,0:T(8,128)(2,1)} async-done(((bf16[4096,128]{1,0:T(8,128)(2,1)}), bf16[8192,128]{1,0:T(8,128)(2,1)}) %all-gather.5.cloned.1.call-update) | async-done | bytes 2097168 | tf_op jit(solution)/shard_map/all_gather | solution.py:27
  79.8 0.0 copy-done
  79.8 2.3 %fusion.11 = f32[128,8192]{1,0:T(8,128)S(1)} fusion(bf16[128,128]{1,0:T(8,128)(2,1)S(1)} %copy-done, bf16[8192,128]{1,0:T(8,128)(2,1)} %all-gather.5.cloned.1.call-done), kind=kOutput, calls=%fused_computation.19 | convolution fusion | flops 268435456 | bytes 6324224 | tf_op jit(solution)/shard_map/dot_general | solution.py:29
  82.1 3.2 %copy.14 = f32[16,8,32,256]{3,2,1,0:T(8,128)} copy(f32[16,8,32,256]{3,1,2,0:T(8,128)S(1)} %bitcast.25) | data formatting | bytes 8388608
  85.3 5.3 %copy.12 = f32[128,16,2,256]{0,3,2,1:T(8,128)} copy(f32[128,16,2,256]{3,1,2,0:T(8,128)} %bitcast.24) | data formatting | bytes 8388608 | tf_op jit(solution)/shard_map/transpose | solution.py:35
  90.6 0.0 copy-start.1
  90.6 4.2 %fusion.9 = (f32[8192]{0:T(1024)S(1)}, f32[128]{0:T(128)S(1)}) fusion(bf16[128,8192]{0,1:T(8,128)(2,1)S(1)} %copy.10, f32[128,16,2,256]{0,3,2,1:T(8,128)} %copy.12, f32[128]{0:T(128)S(1)} %add_rsqrt_fusion, f32[8192]{0:T(1024)S(1)} %convert_element_type.16), kind=kLoop, calls=%fused_computation.12 | loop fusion | flops 7331712 | bytes 6358016 | tf_op jit(solution)/shard_map/reduce_sum | solution.py:41
  94.8 0.0 copy-done.1
  94.8 4.4 %fusion.8 = (bf16[128,8192]{0,1:T(8,128)(2,1)}, bf16[128,8192]{0,1:T(8,128)(2,1)S(1)}) fusion(bf16[128,8192]{0,1:T(8,128)(2,1)S(1)} %copy.10, f32[128,16,2,256]{0,3,2,1:T(8,128)S(1)} %copy-done.1, f32[128]{0:T(128)S(1)} %broadcast_multiply_fusion.1, f32[8192]{0:T(1024)S(1)} %convert_element_type.16, f32[128]{0:T(128)S(1)} %add_rsqrt_fusion), kind=kLoop, calls=%fused_computation.11 | loop fusion | flops 9437184 | bytes 10519552 | tf_op jit(solution)/shard_map/convert_element_type | solution.py:40
  99.2 0.1 copy.11
  99.3 2.6 %convolution_multiply_fusion = f32[8192,128]{1,0:T(8,128)} fusion(bf16[128,8192]{0,1:T(8,128)(2,1)S(1)} %bitcast.22, bf16[128,128]{1,0:T(8,128)(2,1)S(1)} %copy-done), kind=kOutput, calls=%fused_computation | convolution fusion | flops 269484032 | bytes 6324224 | tf_op jit(solution)/shard_map/dot_general | solution.py:44
  102.0 0.0 reduce-scatter.3.cloned.1.call-update
  102.0 0.0 reduce-scatter.5.cloned.1.call-start
  102.0 13.3 %reduce-scatter.3.cloned.1.call-done = f32[4096,128]{1,0:T(8,128)} async-done(((f32[8192,128]{1,0:T(8,128)}), f32[4096,128]{1,0:T(8,128)}) %reduce-scatter.3.cloned.1.call-update) | async-done | bytes 2097168 | tf_op jit(solution)/shard_map/reduce_scatter | solution.py:43
  115.4 0.0 reduce-scatter.5.cloned.1.call-update
  115.4 4.1 %copy.13 = bf16[128,8192]{1,0:T(8,128)(2,1)} copy(bf16[128,8192]{0,1:T(8,128)(2,1)} %get-tuple-element.10) | data formatting | bytes 4194304
  119.5 42.8 %psum.7 = f32[8192]{0:T(1024)} all-reduce(f32[8192]{0:T(1024)S(1)} %broadcast_multiply_fusion), channel_id=1, replica_groups=mesh['node'=16,'local'=2] {'node','local'}, use_global_device_ids=true, to_apply=%region_5.0 | all-reduce | flops 8192 | bytes 65536 | tf_op jit(solution)/shard_map/psum | solution.py:42
  162.3 3.0 %convolution_convert_fusion = bf16[128,128]{1,0:T(8,128)(2,1)} fusion(bf16[128,8192]{0,1:T(8,128)(2,1)S(1)} %bitcast.23, bf16[8192,128]{1,0:T(8,128)(2,1)} %all-gather.5.cloned.1.call-done), kind=kOutput, calls=%fused_computation.15 | convolution fusion | flops 268451840 | bytes 4227072 | tf_op jit(solution)/shard_map/dot_general | solution.py:28
  165.2 34.9 %reduce-scatter.5.cloned.1.call-done = f32[256,128]{1,0:T(8,128)} async-done(((f32[4096,128]{1,0:T(8,128)}), f32[256,128]{1,0:T(8,128)}) %reduce-scatter.5.cloned.1.call-update) | async-done | bytes 131088 | tf_op jit(solution)/shard_map/reduce_scatter | solution.py:52
  (4 shorter events, 0.0 us)
Async XLA Ops:
  7.2 72.6 %copy-start = (bf16[128,128]{1,0:T(8,128)(2,1)S(1)}, bf16[128,128]{1,0:T(8,128)(2,1)}, u32[]{:S(2)}) copy-start(bf16[128,128]{1,0:T(8,128)(2,1)} %param.7) | copy-start | bytes 98308
  7.2 64.9 %copy-start.2 = (bf16[8192]{0:T(1024)(128)(2,1)S(1)}, bf16[8192]{0:T(1024)(128)(2,1)}, u32[]{:S(2)}) copy-start(bf16[8192]{0:T(1024)(128)(2,1)} %param.5) | copy-start | bytes 49156
  7.2 61.6 %all-gather.3.cloned.1.call-start = ((), (), s32[]{:S(2)}) async-start(), calls=%async_computation.2 | async-start | bytes 1114112 | tf_op jit(solution)/shard_map/all_gather | solution.py:21
  7.9 71.8 %all-gather.5.cloned.1.call-start = ((), (), s32[]{:S(2)}) async-start(), calls=%async_computation.3 | async-start | bytes 3145728 | tf_op jit(solution)/shard_map/all_gather | solution.py:27
  68.8 46.5 %reduce-scatter.3.cloned.1.call-start = ((), (), s32[]{:S(2)}) async-start(), calls=%async_computation.4 | async-start | bytes 6291456 | tf_op jit(solution)/shard_map/reduce_scatter | solution.py:43
  90.6 4.2 %copy-start.1 = (f32[128,16,2,256]{0,3,2,1:T(8,128)S(1)}, f32[128,16,2,256]{0,3,2,1:T(8,128)}, u32[]{:S(2)}) copy-start(f32[128,16,2,256]{0,3,2,1:T(8,128)} %copy.12) | copy-start | bytes 12582916
  102.0 98.1 %reduce-scatter.5.cloned.1.call-start = ((), (), s32[]{:S(2)}) async-start(), calls=%async_computation.5 | async-start | bytes 2228224 | tf_op jit(solution)/shard_map/reduce_scatter | solution.py:52
Sparse Core Ops, SparseCore 0:
  10.8 57.9 all-gather.2
  70.3 9.3 all-gather.4
  102.1 13.2 reduce-scatter.2
  118.2 81.8 reduce-scatter.4
where the time goes:
time: 207 us
  waiting for transfers between devices  116 us (56%)
  blocking collectives  42.8 us (21%)
  local copies, waits for them, and re-layouts  16 us (8%)
  between operations  13.8 us (7%)
  other arithmetic  9.68 us (5%)
  matrix products  7.87 us (4%)
    all_gather x1, waiting for transfers between devices, local(): secondary = lax.all_gather(key_weight, 'node', axis=0, tiled=True)  60.8 us
    psum x1, blocking collectives, local(): gain_grad = lax.psum(gain_terms, ('node', 'local'))  42.8 us
    reduce_scatter x1, waiting for transfers between devices, local(): lax.psum_scatter(partial_grad, 'node', scatter_dimension=0, tiled=True)  34.9 us
    reduce_scatter x1, waiting for transfers between devices, local(): lax.psum_scatter(lax.dot_general(permuted, key_cotangent, (((0,), (0,)),...  13.3 us
    unnamed x9, local copies, waits for them, and re-layouts  10.6 us
    all_gather x1, waiting for transfers between devices, local(): whole = lax.all_gather(secondary, 'local', axis=0, tiled=True)  6.53 us
    transpose x1, local copies, waits for them, and re-layouts, local(): dhidden = dpermuted.reshape(tok_rows, locals_count, nodes, rows_dev).tran...  5.32 us
    convert_element_type x1, other arithmetic, local(): token_grad = (rstd * (dnormed - normed * inner)).astype(jnp.bfloat16)  4.4 us
  transfers between devices with their start and end apart: 4, of which 4 were waited for; matrix products, arithmetic and copies ran while one was open for 6% of the time, Pallas kernels for 0%

commit v1 on v0

v1 whole, which is shorter than its diff:
```python
import functools
import math

import jax
import jax.numpy as jnp
from jax import lax
from jax.experimental import pallas as pl
from jax.experimental.pallas import tpu as pltpu
from jax.sharding import PartitionSpec as P

MESH = pl.DeviceIdType.MESH
F32 = jnp.float32
BF16 = jnp.bfloat16


def stream_plan(bits, rows):
    rest = list(range(1, bits))
    if bits == 5 and rows % 256 == 0:
        unit = rows // 8
        sizes = [3 * unit, 3 * unit, 2 * unit]
        orders = [[0, 1, 2, 3, 4], [0, 2, 3, 4, 1], [0, 3, 4, 1, 2]]
    else:
        sizes = [rows // 2, rows // 2]
        orders = [[0] + rest, [0] + rest[::-1]]
    return sizes, orders


def kernel(
    plan, local_count, scale, tok_hbm, gain_ref, w_ref, cot_ref,
    keys_ref, tg_hbm, wg_ref, gg_ref,
    tok, hid, tg, gains, rstds, rowco, gmine, gall, *rest,
):
    sizes, orders = plan
    bits = len(orders[0])
    count = 1 << bits
    streams = len(sizes)
    offs = [sum(sizes[:s]) for s in range(streams)]
    rows, heads = w_ref.shape
    toks, width = tok.shape
    it = iter(rest)
    wbuf = [next(it) for _ in range(streams)]
    acc = [next(it) for _ in range(streams)]
    send = [[next(it) for _ in range(bits)] for _ in range(streams)]
    recv = [[next(it) for _ in range(bits)] for _ in range(streams)]
    (tok_sem, tg_sem, ag_send, ag_recv, rs_send, rs_recv, g_send, g_recv) = list(it)

    me = lax.axis_index("node") * local_count + lax.axis_index("local")
    mine = [(me // (1 << k)) % 2 for k in range(bits)]

    def device(index):
        return (index // local_count, index % local_count)

    def partner(bit):
        return device(me + (1 << bit) * (1 - 2 * mine[bit]))

    def block_of(r):
        total = 0
        for k in range(bits):
            total = total + (1 << k) * ((mine[k] + r // (1 << k)) % 2)
        return total

    def place(s, r):
        total = 0
        for j, k in enumerate(orders[s]):
            total = total + (1 << (bits - 1 - j)) * ((r // (1 << k)) % 2)
        return total

    def columns(i):
        return pl.ds(pl.multiple_of(i * rows, rows), rows)

    def gain_of(i):
        parts = rows // 128
        return jnp.concatenate(
            [gains[pl.ds(i * parts + j, 1), :] for j in range(parts)], axis=1
        )

    chunks = tok_sem.shape[0]
    cw = width // chunks
    tok_copies = [
        pltpu.make_async_copy(
            tok_hbm.at[:, pl.ds(c * cw, cw)], tok.at[:, pl.ds(c * cw, cw)], tok_sem.at[c]
        )
        for c in range(chunks)
    ]
    for copy in tok_copies:
        copy.start()

    barrier = pltpu.get_barrier_semaphore()

    def greet(j, carry):
        pl.semaphore_signal(
            barrier, inc=1, device_id=device((me + j) % count), device_id_type=MESH
        )
        return carry

    lax.fori_loop(1, count, greet, 0)
    for s in range(streams):
        wbuf[s][0] = w_ref[pl.ds(offs[s], sizes[s]), :]
    gains[...] = gain_ref[...].astype(F32)
    pl.semaphore_wait(barrier, count - 1)

    def ag_copy(s, k):
        size = 1 << k
        return pltpu.make_async_remote_copy(
            src_ref=wbuf[s].at[pl.ds(0, size)],
            dst_ref=wbuf[s].at[pl.ds(size, size)],
            send_sem=ag_send.at[s, k],
            recv_sem=ag_recv.at[s, k],
            device_id=partner(orders[s][bits - 1 - k]),
            device_id_type=MESH,
        )

    def ag_step(k):
        for s in range(streams):
            if k:
                ag_copy(s, k - 1).wait_recv()
            if k < bits:
                ag_copy(s, k).start()

    def rs_copy(s, k):
        return pltpu.make_async_remote_copy(
            src_ref=send[s][k],
            dst_ref=recv[s][k],
            send_sem=rs_send.at[s, k],
            recv_sem=rs_recv.at[s, k],
            device_id=partner(orders[s][k]),
            device_id_type=MESH,
        )

    def rs_step(k):
        half = count >> (k + 1)
        for s in range(streams):
            rs_copy(s, k).wait_recv()
            low = half // 2
            if low:
                for p in range(low):
                    send[s][k + 1][p] = (
                        acc[s][low + p] + recv[s][k][low + p].astype(F32)
                    ).astype(BF16)
                rs_copy(s, k + 1).start()
                for p in range(low):
                    acc[s][p] = acc[s][p] + recv[s][k][p].astype(F32)

    ag_step(0)

    squares = jnp.zeros((toks, 128), F32)
    for c in range(chunks):
        tok_copies[c].wait()

        def square(j, total, c=c):
            part = tok[:, pl.ds(pl.multiple_of(c * cw + j * 256, 256), 256)].astype(F32)
            part = part * part
            return total + part[:, :128] + part[:, 128:]

        squares = lax.fori_loop(0, cw // 256, square, squares, unroll=2)
    rstd = lax.rsqrt(jnp.sum(squares, axis=1, keepdims=True) * (1.0 / width) + 1e-05)
    rstds[...] = jnp.broadcast_to(rstd, rstds.shape)

    ag_step(1)

    def weight_terms(flip):
        def body(q, carry):
            r = 2 * q + flip
            i = block_of(r)
            normed = tok[:, columns(i)].astype(F32) * rstds[:, :1]
            hidden = (normed * gain_of(i)).astype(BF16)
            hid[:, columns(i)] = hidden
            terms = lax.dot_general(
                hidden, cot_ref[...], (((0,), (0,)), ((), ())), preferred_element_type=F32
            )
            for s in range(streams):
                part = terms[offs[s]: offs[s] + sizes[s]]
                if flip:
                    send[s][0][place(s, r) - count // 2] = part.astype(BF16)
                else:
                    acc[s][place(s, r)] = part
            return carry

        lax.fori_loop(0, count // 2, body, 0, unroll=2)

    weight_terms(1)
    for s in range(streams):
        rs_copy(s, 0).start()
    ag_step(2)
    weight_terms(0)
    rs_step(0)
    for k in range(3, bits):
        ag_step(k)

    def weights(r):
        return jnp.concatenate([wbuf[s][place(s, r)] for s in range(streams)], axis=0)

    def keys_of(flip, total):
        def body(q, total):
            r = 2 * q + flip
            return total + jnp.dot(
                hid[:, columns(block_of(r))], weights(r), preferred_element_type=F32
            )

        return lax.fori_loop(0, count // 2, body, total, unroll=2)

    total = keys_of(0, jnp.zeros((toks, heads), F32))
    rs_step(1)
    ag_step(bits)
    total = keys_of(1, total)
    keys_ref[...] = total.astype(BF16)
    inner = jnp.sum(total * cot_ref[...].astype(F32), axis=1, keepdims=True) * (1.0 / width)
    back = rstds[:, :1]
    rowco[...] = jnp.broadcast_to(back * back * inner, rowco.shape)
    rs_step(2)

    groups = tg_sem.shape[0]
    gw = width // groups
    per = count // groups

    def tg_copy(g):
        return pltpu.make_async_copy(
            tg.at[:, pl.ds(g * gw, gw)], tg_hbm.at[:, pl.ds(g * gw, gw)], tg_sem.at[g]
        )

    def token_group(g):
        def body(q, carry):
            i = g * per + q
            r = block_of(i)
            dhidden = lax.dot_general(
                cot_ref[...], weights(r), (((1,), (1,)), ((), ())), preferred_element_type=F32
            )
            wide = tok[:, columns(i)].astype(F32)
            tg[:, columns(i)] = (
                dhidden * gain_of(i) * rstds[:, :1] - wide * rowco[:, :1]
            ).astype(BF16)
            return carry

        lax.fori_loop(0, per, body, 0, unroll=2)
        tg_copy(g).start()

    def gain_copy(j):
        return pltpu.make_async_remote_copy(
            src_ref=gmine,
            dst_ref=gall.at[me],
            send_sem=g_send.at[j],
            recv_sem=g_recv.at[j],
            device_id=device((me + j) % count),
            device_id_type=MESH,
        )

    def finish_weight():
        parts = []
        for s in range(streams):
            rs_copy(s, bits - 1).wait_recv()
            parts.append((acc[s][0] + recv[s][bits - 1][0].astype(F32)) * scale)
        grad = jnp.concatenate(parts, axis=0)
        wg_ref[...] = grad
        product = grad * w_ref[...].astype(F32)
        ones = jnp.ones((8, heads), F32)
        sums = lax.dot_general(
            ones, product, (((1,), (1,)), ((), ())),
            precision=lax.Precision.HIGHEST, preferred_element_type=F32,
        )
        own = sums[:1] / gain_of(me)
        gmine[...] = own
        gall[me] = own

        def give(j, carry):
            gain_copy(j).start()
            return carry

        lax.fori_loop(1, count, give, 0)

    steps = [functools.partial(rs_step, k) for k in range(3, bits - 1)] + [finish_weight]
    for g in range(groups):
        token_group(g)
        if g % 2 == 0 and steps:
            steps.pop(0)()
    for step in steps:
        step()

    def taken(j, carry):
        gain_copy(j).wait_recv()
        gain_copy(j).wait_send()
        return carry

    lax.fori_loop(1, count, taken, 0)
    parts = rows // 128
    for b in range(count):
        for j in range(parts):
            gg_ref[b * parts + j: b * parts + j + 1, :] = gall[b, :, j * 128: (j + 1) * 128]
    for s in range(streams):
        for k in range(bits):
            ag_copy(s, k).wait_send()
            rs_copy(s, k).wait_send()
    for g in range(groups):
        tg_copy(g).wait()


def fused(local_count, count, scale, tokens, norm_gain, key_weight, key_cotangent):
    rows, heads = key_weight.shape
    toks, width = tokens.shape
    bits = count.bit_length() - 1
    plan = stream_plan(bits, rows)
    sizes, _ = plan
    vmem = pl.BlockSpec(memory_space=pltpu.VMEM)
    hbm = pl.BlockSpec(memory_space=pl.ANY)
    stages = [
        pltpu.VMEM((count >> (k + 1), size, heads), BF16) for size in sizes for k in range(bits)
    ]
    keys, tg, wg, gg = pl.pallas_call(
        functools.partial(kernel, plan, local_count, scale),
        out_shape=(
            jax.ShapeDtypeStruct((toks, heads), BF16),
            jax.ShapeDtypeStruct((toks, width), BF16),
            jax.ShapeDtypeStruct((rows, heads), F32),
            jax.ShapeDtypeStruct((width // 128, 128), F32),
        ),
        in_specs=[hbm, vmem, vmem, vmem],
        out_specs=(vmem, hbm, vmem, vmem),
        scratch_shapes=[
            pltpu.VMEM((toks, width), BF16),
            pltpu.VMEM((toks, width), BF16),
            pltpu.VMEM((toks, width), BF16),
            pltpu.VMEM((width // 128, 128), F32),
            pltpu.VMEM((toks, 128), F32),
            pltpu.VMEM((toks, 128), F32),
            pltpu.VMEM((1, rows), F32),
            pltpu.VMEM((count, 1, rows), F32),
        ]
        + [pltpu.VMEM((count, size, heads), BF16) for size in sizes]
        + [pltpu.VMEM((count // 2, size, heads), F32) for size in sizes]
        + stages
        + stages
        + [
            pltpu.SemaphoreType.DMA((4,)),
            pltpu.SemaphoreType.DMA((8,)),
            pltpu.SemaphoreType.DMA((len(sizes), bits)),
            pltpu.SemaphoreType.DMA((len(sizes), bits)),
            pltpu.SemaphoreType.DMA((len(sizes), bits)),
            pltpu.SemaphoreType.DMA((len(sizes), bits)),
            pltpu.SemaphoreType.DMA((count,)),
            pltpu.SemaphoreType.DMA((count,)),
        ],
        compiler_params=pltpu.CompilerParams(
            collective_id=0, has_side_effects=True, vmem_limit_bytes=48 * 2**20
        ),
        cost_estimate=pl.CostEstimate(
            flops=6 * toks * width * heads, bytes_accessed=4 * toks * width, transcendentals=0
        ),
    )(tokens, norm_gain.reshape(width // 128, 128), key_weight, key_cotangent)
    return keys, tg, wg, gg.reshape(width)


def plain(scale, tokens, norm_gain, key_weight, key_cotangent):
    gain_wide = norm_gain.astype(F32)
    wide = tokens.astype(F32)
    rstd = lax.rsqrt(jnp.mean(wide * wide, axis=1, keepdims=True) + 1e-05)
    normed = wide * rstd
    hidden = (normed * gain_wide).astype(BF16)
    whole = lax.all_gather(key_weight, ("node", "local"), axis=0, tiled=True)
    keys = jnp.dot(hidden, whole, preferred_element_type=F32).astype(BF16)
    dhidden = lax.dot_general(
        key_cotangent, whole, (((1,), (1,)), ((), ())), preferred_element_type=F32
    )
    dnormed = dhidden * gain_wide
    inner = jnp.mean(dnormed * normed, axis=1, keepdims=True)
    token_grad = (rstd * (dnormed - normed * inner)).astype(BF16)
    gain_grad = lax.psum(jnp.sum(dhidden * normed, axis=0) * scale, ("node", "local"))
    terms = lax.dot_general(
        hidden, key_cotangent, (((0,), (0,)), ((), ())), preferred_element_type=F32
    )
    weight_grad = lax.psum_scatter(
        terms * scale, ("node", "local"), scatter_dimension=0, tiled=True
    )
    return keys, token_grad, weight_grad, gain_grad


def solution(mesh):
    local_count = mesh.shape["local"]
    count = mesh.shape["node"] * local_count

    def local(tokens, norm_gain, key_weight, key_cotangent):
        scale = 1.0 / math.sqrt(tokens.shape[0] * count)
        if key_weight.shape[0] % 128 == 0 and count & (count - 1) == 0 and count >= 16:
            return fused(
                local_count, count, scale, tokens, norm_gain, key_weight, key_cotangent
            )
        return plain(scale, tokens, norm_gain, key_weight, key_cotangent)

    placed = P(("node", "local"), None)
    return jax.shard_map(
        local,
        mesh=mesh,
        in_specs=(placed, P(), placed, placed),
        out_specs=(placed, placed, placed, P()),
        check_vma=False,
    )
```

time: 207 us -> 52.4 us (0.25)
  waiting for transfers between devices: 116 us -> 0 us
  Pallas kernels: 0 us -> 44.3 us
  blocking collectives: 42.8 us -> 0 us
  between operations: 13.8 us -> 0.65 us
  other arithmetic: 9.68 us -> 0 us
  local copies, waits for them, and re-layouts: 16 us -> 7.1 us
  matrix products: 7.87 us -> 0 us
    all_gather x2 -> x0, waiting for transfers between devices: 67.3 us -> none  [the longest x1 60.8 us: local(): secondary = lax.all_gather(key_weight, 'node', axis=0, tiled=True)]
    reduce_scatter x2 -> x0, waiting for transfers between devices: 48.2 us -> none  [the longest x1 34.9 us: local(): lax.psum_scatter(partial_grad, 'node', scatter_dimension=0, tiled=True)]
    pallas_call x0 -> x1, Pallas kernels: none -> 44.3 us  [fused(): pl.pallas_call(functools.partial(kernel, plan, local_count, scale), out_s...]
    psum x1 -> x0, blocking collectives: 42.8 us -> none  [local(): gain_grad = lax.psum(gain_terms, ('node', 'local'))]
    dot_general x3 -> x0, matrix products: 7.87 us -> none  [the longest x1 2.97 us: local(): keys_wide = jnp.dot(permuted, whole, preferred_element_type=jnp.float32)]
    transpose x2 -> x0, local copies, waits for them, and re-layouts: 5.46 us -> none  [the longest x1 5.32 us: local(): dhidden = dpermuted.reshape(tok_rows, locals_count, nodes, rows_dev).tran...]
    reduce_sum x2 -> x0, other arithmetic: 5.25 us -> none  [the longest x1 4.16 us: local(): gain_terms = jnp.sum(dhidden * normed, axis=0) * scale]
    convert_element_type x2 -> x0, other arithmetic: 4.41 us -> none  [the longest x1 4.4 us: local(): token_grad = (rstd * (dnormed - normed * inner)).astype(jnp.bfloat16)]
  transfers between devices with their start and end apart: 4 -> 0, of which waited for: 4 -> 0; matrix products, arithmetic and copies ran while one was open for 6% -> 0% of each run, Pallas kernels for 0% -> 0%
where the time goes in v1:
time: 52.4 us; the launch traced here: 52.1 us
  Pallas kernels  44.3 us (85%)
  local copies, waits for them, and re-layouts  7.1 us (14%)
  between operations  0.65 us (1%)
    pallas_call x1, Pallas kernels, fused(): pl.pallas_call(functools.partial(kernel, plan, local_count, scale), out_s...  44.3 us
    unnamed x12, local copies, waits for them, and re-layouts  7.1 us

profile of v1, /device:TPU:0, one launch (start us, length us, event | category | flops | bytes accessed | tf_op | source)
XLA Modules:
  0.0 52.1 jit_solution(16681889382100913796)
XLA Ops:
  0.6 0.0 copy-start
  0.6 1.6 %copy-done = bf16[128,8192]{1,0:T(8,128)(2,1)S(1)} copy-done((bf16[128,8192]{1,0:T(8,128)(2,1)S(1)}, bf16[128,8192]{1,0:T(8,128)(2,1)}, u32[]{:S(2)}) %copy-start) | copy-done | bytes 2097176
  2.2 0.0 copy-start.1
  2.2 0.8 %copy-done.1 = bf16[256,128]{1,0:T(8,128)(2,1)S(1)} copy-done((bf16[256,128]{1,0:T(8,128)(2,1)S(1)}, bf16[256,128]{1,0:T(8,128)(2,1)}, u32[]{:S(2)}) %copy-start.1) | copy-done | bytes 65560
  3.1 0.0 copy-start.2
  3.1 0.8 %copy-done.2 = bf16[128,128]{1,0:T(8,128)(2,1)S(1)} copy-done((bf16[128,128]{1,0:T(8,128)(2,1)S(1)}, bf16[128,128]{1,0:T(8,128)(2,1)}, u32[]{:S(2)}) %copy-start.2) | copy-done | bytes 32792
  3.8 0.0 copy-start.3
  3.8 0.7 %copy-done.3 = bf16[8192]{0:T(1024)(128)(2,1)S(1)} copy-done((bf16[8192]{0:T(1024)(128)(2,1)S(1)}, bf16[8192]{0:T(1024)(128)(2,1)}, u32[]{:S(2)}) %copy-start.3) | copy-done | bytes 16408
  4.5 44.3 %shard_map.75 = (bf16[128,128]{1,0:T(8,128)(2,1)S(1)}, bf16[128,8192]{1,0:T(8,128)(2,1)S(1)}, f32[256,128]{1,0:T(8,128)S(1)}, f32[64,128]{1,0:T(8,128)S(1)}) custom-call(bf16[128,8192]{1,0:T(8,128)(2,1)S(1)} %copy-done, bf16[64,128]{1,0:T(8,128)(2,1)S(1)} %bitcast.3, bf16[256,128]{1,0:T(8,128)(2,1)S(1)} %copy-done.1, bf16[128,128]{1,0:T(8,128)(2,1)S(1)} %copy-done.2), custom_call_target="tpu_custom_call" | custom-call | flops 805306368 | bytes 4194304 | tf_op jit(solution)/shard_map/pallas_call | solution.py:307
  48.9 0.6 %copy.12 = bf16[128,128]{1,0:T(8,128)(2,1)} copy(bf16[128,128]{1,0:T(8,128)(2,1)S(1)} %get-tuple-element.16) | data formatting | bytes 65536
  49.5 1.3 %copy.13 = bf16[128,8192]{1,0:T(8,128)(2,1)} copy(bf16[128,8192]{1,0:T(8,128)(2,1)S(1)} %get-tuple-element.17) | data formatting | bytes 4194304
  50.8 0.7 %copy.14 = f32[256,128]{1,0:T(8,128)} copy(f32[256,128]{1,0:T(8,128)S(1)} %get-tuple-element.18) | data formatting | bytes 262144
  51.5 0.6 %copy.15 = f32[8192]{0:T(1024)} copy(f32[8192]{0:T(1024)S(1)} %bitcast.2) | data formatting | bytes 65536
Async XLA Ops:
  0.6 1.6 %copy-start = (bf16[128,8192]{1,0:T(8,128)(2,1)S(1)}, bf16[128,8192]{1,0:T(8,128)(2,1)}, u32[]{:S(2)}) copy-start(bf16[128,8192]{1,0:T(8,128)(2,1)} %tok_hbm.1) | copy-start | bytes 6291460
  2.2 0.8 %copy-start.1 = (bf16[256,128]{1,0:T(8,128)(2,1)S(1)}, bf16[256,128]{1,0:T(8,128)(2,1)}, u32[]{:S(2)}) copy-start(bf16[256,128]{1,0:T(8,128)(2,1)} %w_ref.1) | copy-start | bytes 196612
  3.1 0.8 %copy-start.2 = (bf16[128,128]{1,0:T(8,128)(2,1)S(1)}, bf16[128,128]{1,0:T(8,128)(2,1)}, u32[]{:S(2)}) copy-start(bf16[128,128]{1,0:T(8,128)(2,1)} %cot_ref.1) | copy-start | bytes 98308
  3.8 0.7 %copy-start.3 = (bf16[8192]{0:T(1024)(128)(2,1)S(1)}, bf16[8192]{0:T(1024)(128)(2,1)}, u32[]{:S(2)}) copy-start(bf16[8192]{0:T(1024)(128)(2,1)} %param.5) | copy-start | bytes 49156

commit v2 on v1

v2 whole, which is shorter than its diff:
```python
import functools
import math

import jax
import jax.numpy as jnp
from jax import lax
from jax.experimental import pallas as pl
from jax.experimental.pallas import tpu as pltpu
from jax.sharding import PartitionSpec as P

MESH = pl.DeviceIdType.MESH
F32 = jnp.float32
BF16 = jnp.bfloat16


def stream_plan(bits):
    rest = list(range(1, bits))
    if bits == 5:
        return [3, 3, 2], [[0, 1, 2, 3, 4], [0, 2, 3, 4, 1], [0, 3, 4, 1, 2]]
    return [4, 4], [[0] + rest, [0] + rest[::-1]]


def kernel(
    plan, local_count, scale, tok_hbm, gain_hbm, w_hbm, cot_hbm,
    keys_hbm, tg_hbm, wg_hbm, gg_hbm,
    keys_ref, tg_ref, wg_ref, gg_ref, tok, gain_ref, w_ref, cot_ref, hid, back, gains, rstds, rowco, gmine, gall, *rest,
):
    shares, orders = plan
    bits = len(orders[0])
    count = 1 << bits
    streams = len(shares)
    rows, heads = w_ref.shape
    toks, width = tok.shape
    wsize = [n * rows // 8 for n in shares]
    woff = [sum(wsize[:s]) for s in range(streams)]
    gsize = [n * heads // 8 for n in shares]
    goff = [sum(gsize[:s]) for s in range(streams)]
    it = iter(rest)
    wbuf = [next(it) for _ in range(streams)]
    acc = [next(it) for _ in range(streams)]
    send = [[next(it) for _ in range(bits)] for _ in range(streams)]
    recv = [[next(it) for _ in range(bits)] for _ in range(streams)]
    (tok_sem, in_sem, out_sem, ag_send, ag_recv, rs_send, rs_recv, g_send, g_recv) = list(it)

    me = lax.axis_index("node") * local_count + lax.axis_index("local")
    mine = [(me // (1 << k)) % 2 for k in range(bits)]

    def device(index):
        return (index // local_count, index % local_count)

    def partner(bit):
        return device(me + (1 << bit) * (1 - 2 * mine[bit]))

    def block_of(r):
        total = 0
        for k in range(bits):
            total = total + (1 << k) * ((mine[k] + r // (1 << k)) % 2)
        return total

    def place(s, r):
        total = 0
        for j, k in enumerate(orders[s]):
            total = total + (1 << (bits - 1 - j)) * ((r // (1 << k)) % 2)
        return total

    def columns(i):
        return pl.ds(pl.multiple_of(i * rows, rows), rows)

    parts = rows // 128

    def gain_of(i):
        return jnp.concatenate(
            [gains[pl.ds(i * parts + j, 1), :] for j in range(parts)], axis=1
        )

    def across(ref):
        return jnp.concatenate([ref[...]] * parts, axis=1)

    w_copy = pltpu.make_async_copy(w_hbm, w_ref, in_sem.at[0])
    cot_copy = pltpu.make_async_copy(cot_hbm, cot_ref, in_sem.at[1])
    gain_copy_in = pltpu.make_async_copy(gain_hbm, gain_ref, in_sem.at[2])
    chunks = tok_sem.shape[0]
    cw = width // chunks
    tok_copies = [
        pltpu.make_async_copy(
            tok_hbm.at[:, pl.ds(c * cw, cw)], tok.at[:, pl.ds(c * cw, cw)], tok_sem.at[c]
        )
        for c in range(chunks)
    ]
    for copy in [w_copy] + tok_copies + [cot_copy, gain_copy_in]:
        copy.start()

    barrier = pltpu.get_barrier_semaphore()

    def greet(j, carry):
        pl.semaphore_signal(
            barrier, inc=1, device_id=device((me + j) % count), device_id_type=MESH
        )
        return carry

    lax.fori_loop(1, count, greet, 0)
    w_copy.wait()
    for s in range(streams):
        wbuf[s][0] = w_ref[pl.ds(woff[s], wsize[s]), :]
    pl.semaphore_wait(barrier, count - 1)

    def ag_copy(s, k):
        size = 1 << k
        return pltpu.make_async_remote_copy(
            src_ref=wbuf[s].at[pl.ds(0, size)],
            dst_ref=wbuf[s].at[pl.ds(size, size)],
            send_sem=ag_send.at[s, k],
            recv_sem=ag_recv.at[s, k],
            device_id=partner(orders[s][bits - 1 - k]),
            device_id_type=MESH,
        )

    def ag_step(k):
        for s in range(streams):
            if k:
                ag_copy(s, k - 1).wait_recv()
            if k < bits:
                ag_copy(s, k).start()

    def rs_copy(s, k):
        return pltpu.make_async_remote_copy(
            src_ref=send[s][k],
            dst_ref=recv[s][k],
            send_sem=rs_send.at[s, k],
            recv_sem=rs_recv.at[s, k],
            device_id=partner(orders[s][k]),
            device_id_type=MESH,
        )

    def rs_step(k):
        half = count >> (k + 1)
        low = half // 2
        for s in range(streams):
            rs_copy(s, k).wait_recv()
            for p in range(low):
                send[s][k + 1][p] = (
                    acc[s][low + p] + recv[s][k][low + p].astype(F32)
                ).astype(BF16)
            rs_copy(s, k + 1).start()
        for s in range(streams):
            for p in range(low):
                acc[s][p] = acc[s][p] + recv[s][k][p].astype(F32)

    ag_step(0)

    squares = jnp.zeros((toks, 128), F32)
    for c in range(chunks):
        tok_copies[c].wait()

        def square(j, total, c=c):
            part = tok[:, pl.ds(pl.multiple_of(c * cw + j * 512, 512), 512)].astype(F32)
            part = part * part
            return total + (
                (part[:, :128] + part[:, 128:256]) + (part[:, 256:384] + part[:, 384:])
            )

        squares = lax.fori_loop(0, cw // 512, square, squares)
    rstd = lax.rsqrt(jnp.sum(squares, axis=1, keepdims=True) * (1.0 / width) + 1e-05)
    rstds[...] = jnp.broadcast_to(rstd, rstds.shape)
    gain_copy_in.wait()
    gains[...] = gain_ref[...].astype(F32)
    cot_copy.wait()

    ag_step(1)

    cot_t = cot_ref[...].T

    def weight_terms(flip):
        def body(q, carry):
            r = 2 * q + flip
            i = block_of(r)
            normed = tok[:, columns(i)].astype(F32) * across(rstds)
            hidden = (normed * gain_of(i)).astype(BF16)
            hid[:, columns(i)] = hidden
            terms = jnp.dot(cot_t, hidden, preferred_element_type=F32)
            for s in range(streams):
                part = terms[goff[s]: goff[s] + gsize[s]]
                if flip:
                    send[s][0][place(s, r) - count // 2] = part.astype(BF16)
                else:
                    acc[s][place(s, r)] = part
            return carry

        lax.fori_loop(0, count // 2, body, 0, unroll=4)

    weight_terms(1)
    for s in range(streams):
        rs_copy(s, 0).start()
    ag_step(2)
    weight_terms(0)
    rs_step(0)
    for k in range(3, bits):
        ag_step(k)

    def weight_pass(flip, begin, end, total):
        def body(q, total):
            r = 2 * q + flip
            i = block_of(r)
            block = jnp.concatenate([wbuf[s][place(s, r)] for s in range(streams)], axis=0)
            dhidden = lax.dot_general(
                cot_ref[...], block, (((1,), (1,)), ((), ())), preferred_element_type=F32
            )
            back[:, columns(i)] = dhidden * gain_of(i) * across(rstds)
            return total + jnp.dot(hid[:, columns(i)], block, preferred_element_type=F32)

        return lax.fori_loop(begin, end, body, total, unroll=4)

    half, quarter = count // 2, count // 4
    rs_step(1)
    total = weight_pass(0, 0, half, jnp.zeros((toks, heads), F32))
    rs_step(2)
    ag_step(bits)
    total = weight_pass(1, 0, quarter, total)
    for k in range(3, bits - 1):
        rs_step(k)
    total = weight_pass(1, quarter, half, total)

    def gain_copy(j):
        return pltpu.make_async_remote_copy(
            src_ref=gmine,
            dst_ref=gall.at[me],
            send_sem=g_send.at[j],
            recv_sem=g_recv.at[j],
            device_id=device((me + j) % count),
            device_id_type=MESH,
        )

    pieces = []
    for s in range(streams):
        rs_copy(s, bits - 1).wait_recv()
        pieces.append((acc[s][0] + recv[s][bits - 1][0].astype(F32)) * scale)
    grad = jnp.concatenate(pieces, axis=0).T
    product = grad * w_ref[...].astype(F32)
    sums = lax.dot_general(
        jnp.ones((8, heads), F32), product, (((1,), (1,)), ((), ())),
        precision=lax.Precision.HIGHEST, preferred_element_type=F32,
    )
    own = sums[:1] / gain_of(me)
    gmine[...] = own
    gall[me] = own

    def give(j, carry):
        gain_copy(j).start()
        return carry

    lax.fori_loop(1, count, give, 0)
    wg_ref[...] = grad
    keys_ref[...] = total.astype(BF16)
    outs = [
        pltpu.make_async_copy(wg_ref, wg_hbm, out_sem.at[0]),
        pltpu.make_async_copy(keys_ref, keys_hbm, out_sem.at[1]),
    ]
    for copy in outs:
        copy.start()
    inner = jnp.sum(total * cot_ref[...].astype(F32), axis=1, keepdims=True) * (1.0 / width)
    rowco[...] = rstds[...] * rstds[...] * inner

    def token_part(i, carry):
        tg_ref[:, columns(i)] = (
            back[:, columns(i)] - tok[:, columns(i)].astype(F32) * across(rowco)
        ).astype(BF16)
        return carry

    for g in range(chunks):
        lax.fori_loop(
            g * count // chunks, (g + 1) * count // chunks, token_part, 0, unroll=2
        )
        outs.append(
            pltpu.make_async_copy(
                tg_ref.at[:, pl.ds(g * cw, cw)], tg_hbm.at[:, pl.ds(g * cw, cw)],
                out_sem.at[3 + g],
            )
        )
        outs[-1].start()

    def taken(j, carry):
        gain_copy(j).wait_recv()
        gain_copy(j).wait_send()
        return carry

    lax.fori_loop(1, count, taken, 0)
    for b in range(count):
        for j in range(parts):
            gg_ref[b * parts + j: b * parts + j + 1, :] = gall[b, :, j * 128: (j + 1) * 128]
    outs.append(pltpu.make_async_copy(gg_ref, gg_hbm, out_sem.at[2]))
    outs[-1].start()
    for s in range(streams):
        for k in range(bits):
            ag_copy(s, k).wait_send()
            rs_copy(s, k).wait_send()
    for copy in outs:
        copy.wait()


def hand_out(*refs):
    sems = refs[-1]
    pairs = (len(refs) - 1) // 2
    copies = [
        pltpu.make_async_copy(refs[n], refs[pairs + n], sems.at[n]) for n in range(pairs)
    ]
    for copy in copies:
        copy.start()
    for copy in copies:
        copy.wait()


def fused(local_count, count, scale, tokens, norm_gain, key_weight, key_cotangent):
    rows, heads = key_weight.shape
    toks, width = tokens.shape
    bits = count.bit_length() - 1
    plan = stream_plan(bits)
    shares, _ = plan
    hbm = pl.BlockSpec(memory_space=pltpu.HBM)
    anywhere = pl.BlockSpec(memory_space=pl.ANY)
    stages = [
        pltpu.VMEM((count >> (k + 1), n * heads // 8, rows), BF16)
        for n in shares
        for k in range(bits)
    ]
    shapes = (
        jax.ShapeDtypeStruct((toks, heads), BF16),
        jax.ShapeDtypeStruct((toks, width), BF16),
        jax.ShapeDtypeStruct((rows, heads), F32),
        jax.ShapeDtypeStruct((width // 128, 128), F32),
    )
    results = pl.pallas_call(
        functools.partial(kernel, plan, local_count, scale),
        out_shape=shapes,
        in_specs=[hbm] * 4,
        out_specs=[anywhere] * 4,
        scratch_shapes=[pltpu.VMEM(shape.shape, shape.dtype) for shape in shapes]
        + [
            pltpu.VMEM((toks, width), BF16),
            pltpu.VMEM((width // 128, 128), BF16),
            pltpu.VMEM((rows, heads), BF16),
            pltpu.VMEM((toks, heads), BF16),
            pltpu.VMEM((toks, width), BF16),
            pltpu.VMEM((toks, width), F32),
            pltpu.VMEM((width // 128, 128), F32),
            pltpu.VMEM((toks, 128), F32),
            pltpu.VMEM((toks, 128), F32),
            pltpu.VMEM((1, rows), F32),
            pltpu.VMEM((count, 1, rows), F32),
        ]
        + [pltpu.VMEM((count, n * rows // 8, heads), BF16) for n in shares]
        + [pltpu.VMEM((count // 2, n * heads // 8, rows), F32) for n in shares]
        + stages
        + stages
        + [
            pltpu.SemaphoreType.DMA((4,)),
            pltpu.SemaphoreType.DMA((3,)),
            pltpu.SemaphoreType.DMA((7,)),
            pltpu.SemaphoreType.DMA((len(shares), bits)),
            pltpu.SemaphoreType.DMA((len(shares), bits)),
            pltpu.SemaphoreType.DMA((len(shares), bits)),
            pltpu.SemaphoreType.DMA((len(shares), bits)),
            pltpu.SemaphoreType.DMA((count,)),
            pltpu.SemaphoreType.DMA((count,)),
        ],
        compiler_params=pltpu.CompilerParams(
            collective_id=0, has_side_effects=True, vmem_limit_bytes=58 * 2**20
        ),
        cost_estimate=pl.CostEstimate(
            flops=6 * toks * width * heads, bytes_accessed=4 * toks * width, transcendentals=0
        ),
    )(tokens, norm_gain.reshape(width // 128, 128), key_weight, key_cotangent)
    keys, tg, wg, gg = pl.pallas_call(
        hand_out,
        out_shape=shapes,
        in_specs=[anywhere] * 4,
        out_specs=[hbm] * 4,
        scratch_shapes=[pltpu.SemaphoreType.DMA((4,))],
        compiler_params=pltpu.CompilerParams(vmem_limit_bytes=58 * 2**20),
        cost_estimate=pl.CostEstimate(
            flops=0, bytes_accessed=4 * toks * width, transcendentals=0
        ),
    )(*results)
    return keys, tg, wg, gg.reshape(width)


def plain(scale, tokens, norm_gain, key_weight, key_cotangent):
    gain_wide = norm_gain.astype(F32)
    wide = tokens.astype(F32)
    rstd = lax.rsqrt(jnp.mean(wide * wide, axis=1, keepdims=True) + 1e-05)
    normed = wide * rstd
    hidden = (normed * gain_wide).astype(BF16)
    whole = lax.all_gather(key_weight, ("node", "local"), axis=0, tiled=True)
    keys = jnp.dot(hidden, whole, preferred_element_type=F32).astype(BF16)
    dhidden = lax.dot_general(
        key_cotangent, whole, (((1,), (1,)), ((), ())), preferred_element_type=F32
    )
    dnormed = dhidden * gain_wide
    inner = jnp.mean(dnormed * normed, axis=1, keepdims=True)
    token_grad = (rstd * (dnormed - normed * inner)).astype(BF16)
    gain_grad = lax.psum(jnp.sum(dhidden * normed, axis=0) * scale, ("node", "local"))
    terms = lax.dot_general(
        hidden, key_cotangent, (((0,), (0,)), ((), ())), preferred_element_type=F32
    )
    weight_grad = lax.psum_scatter(
        terms * scale, ("node", "local"), scatter_dimension=0, tiled=True
    )
    return keys, token_grad, weight_grad, gain_grad


def solution(mesh):
    local_count = mesh.shape["local"]
    count = mesh.shape["node"] * local_count

    def local(tokens, norm_gain, key_weight, key_cotangent):
        scale = 1.0 / math.sqrt(tokens.shape[0] * count)
        if key_weight.shape[0] % 128 == 0 and count & (count - 1) == 0 and count >= 16:
            return fused(
                local_count, count, scale, tokens, norm_gain, key_weight, key_cotangent
            )
        return plain(scale, tokens, norm_gain, key_weight, key_cotangent)

    placed = P(("node", "local"), None)
    return jax.shard_map(
        local,
        mesh=mesh,
        in_specs=(placed, P(), placed, placed),
        out_specs=(placed, placed, placed, P()),
        check_vma=False,
    )
```

time: 52.4 us -> 115 us (2.19)
  Pallas kernels: 44.3 us -> 114 us
  local copies, waits for them, and re-layouts: 7.1 us -> 0 us
    pallas_call x0 -> x1, Pallas kernels: none -> 70.6 us  [fused(): pl.pallas_call(hand_out, out_shape=shapes, in_specs=[anywhere] * 4, out_s...]
    unnamed x12 -> x0, local copies, waits for them, and re-layouts: 7.1 us -> none
    pallas_call x1, Pallas kernels: 44.3 us -> 43.2 us  [fused(): pl.pallas_call(functools.partial(kernel, plan, local_count, scale), out_s...]
where the time goes in v2:
time: 115 us; the launch traced here: 114 us
  Pallas kernels  114 us (99%)
    pallas_call x1, Pallas kernels, fused(): pl.pallas_call(hand_out, out_shape=shapes, in_specs=[anywhere] * 4, out_s...  70.6 us
    pallas_call x1, Pallas kernels, fused(): pl.pallas_call(functools.partial(kernel, plan, local_count, scale), out_s...  43.2 us

profile of v2, /device:TPU:0, one launch (start us, length us, event | category | flops | bytes accessed | tf_op | source)
XLA Modules:
  0.0 114.4 jit_solution(981619934806389010)
XLA Ops:
  0.6 43.2 %shard_map.75 = (bf16[128,128]{1,0:T(8,128)(2,1)}, bf16[128,8192]{1,0:T(8,128)(2,1)}, f32[256,128]{1,0:T(8,128)}, f32[64,128]{1,0:T(8,128)}) custom-call(bf16[128,8192]{1,0:T(8,128)(2,1)} %tok_hbm.1, bf16[64,128]{1,0:T(8,128)(2,1)} %bitcast.3, bf16[256,128]{1,0:T(8,128)(2,1)} %w_hbm.1, bf16[128,128]{1,0:T(8,128)(2,1)} %cot_hbm.1), custom_call_target="tpu_custom_call" | custom-call | flops 805306368 | bytes 4194304 | tf_op jit(solution)/shard_map/pallas_call | solution.py:331
  43.8 70.6 %shard_map.76 = (bf16[128,128]{1,0:T(8,128)(2,1)}, bf16[128,8192]{1,0:T(8,128)(2,1)}, f32[256,128]{1,0:T(8,128)}, f32[64,128]{1,0:T(8,128)}) custom-call(bf16[128,128]{1,0:T(8,128)(2,1)} %get-tuple-element.12.refs_0_, bf16[128,8192]{1,0:T(8,128)(2,1)} %get-tuple-element.13.refs_1_, f32[256,128]{1,0:T(8,128)} %get-tuple-element.14.refs_2_, ...), custom_call_target="tpu_custom_call" | custom-call | bytes 4194304 | tf_op jit(solution)/shard_map/pallas_call | solution.py:372

commit v3 on v2

--- a/solution.py
+++ b/solution.py
@@ -20,10 +20,15 @@
     return [4, 4], [[0] + rest, [0] + rest[::-1]]
 
 
+def gain_groups(bits):
+    rest = list(range(1, bits))
+    return [rest[max(0, n - 2): n] for n in range(len(rest), 0, -2)] + [[0]]
+
+
 def kernel(
     plan, local_count, scale, tok_hbm, gain_hbm, w_hbm, cot_hbm,
     keys_hbm, tg_hbm, wg_hbm, gg_hbm,
-    keys_ref, tg_ref, wg_ref, gg_ref, tok, gain_ref, w_ref, cot_ref, hid, back, gains, rstds, rowco, gmine, gall, *rest,
+    keys_ref, tg_ref, wg_ref, gg_ref, tok, gain_ref, w_ref, cot_ref, hid, back, gains, rstds, rowco, gall, *rest,
 ):
     shares, orders = plan
     bits = len(orders[0])
@@ -38,9 +43,13 @@
     it = iter(rest)
     wbuf = [next(it) for _ in range(streams)]
     acc = [next(it) for _ in range(streams)]
-    send = [[next(it) for _ in range(bits)] for _ in range(streams)]
-    recv = [[next(it) for _ in range(bits)] for _ in range(streams)]
-    (tok_sem, in_sem, out_sem, ag_send, ag_recv, rs_send, rs_recv, g_send, g_recv) = list(it)
+    send = [[None] + [next(it) for _ in range(1, bits)] for _ in range(streams)]
+    recv = [[None] + [next(it) for _ in range(1, bits)] for _ in range(streams)]
+    (sent, came) = next(it), next(it)
+    (
+        tok_sem, in_sem, out_sem, ag_send, ag_recv, fw_send, fw_recv,
+        pair_send, pair_recv, rs_send, rs_recv, g_send, g_recv,
+    ) = list(it)
 
     me = lax.axis_index("node") * local_count + lax.axis_index("local")
     mine = [(me // (1 << k)) % 2 for k in range(bits)]
@@ -48,8 +57,8 @@
     def device(index):
         return (index // local_count, index % local_count)
 
-    def partner(bit):
-        return device(me + (1 << bit) * (1 - 2 * mine[bit]))
+    def partner(r):
+        return device(block_of(r))
 
     def block_of(r):
         total = 0
@@ -62,6 +71,9 @@
         for j, k in enumerate(orders[s]):
             total = total + (1 << (bits - 1 - j)) * ((r // (1 << k)) % 2)
         return total
+
+    def at_place(s, p):
+        return sum(((p >> (bits - 1 - j)) & 1) << k for j, k in enumerate(orders[s]))
 
     def columns(i):
         return pl.ds(pl.multiple_of(i * rows, rows), rows)
@@ -92,17 +104,16 @@
 
     barrier = pltpu.get_barrier_semaphore()
 
-    def greet(j, carry):
-        pl.semaphore_signal(
-            barrier, inc=1, device_id=device((me + j) % count), device_id_type=MESH
-        )
-        return carry
-
-    lax.fori_loop(1, count, greet, 0)
+    groups = [high for high in gain_groups(bits)]
+    friends = sorted({1 << k for k in range(bits)} | {sum(1 << k for k in g) for g in groups})
+    for r in friends:
+        pl.semaphore_signal(barrier, inc=1, device_id=partner(r), device_id_type=MESH)
     w_copy.wait()
     for s in range(streams):
         wbuf[s][0] = w_ref[pl.ds(woff[s], wsize[s]), :]
-    pl.semaphore_wait(barrier, count - 1)
+    pl.semaphore_wait(barrier, len(friends))
+
+    half, quarter = count // 2, count // 4
 
     def ag_copy(s, k):
         size = 1 << k
@@ -111,7 +122,18 @@
             dst_ref=wbuf[s].at[pl.ds(size, size)],
             send_sem=ag_send.at[s, k],
             recv_sem=ag_recv.at[s, k],
-            device_id=partner(orders[s][bits - 1 - k]),
+            device_id=partner(1 << orders[s][bits - 1 - k]),
+            device_id_type=MESH,
+        )
+
+    def forward(s, k):
+        start, size = (1 << k) // 2, max(1, (1 << k) // 2)
+        return pltpu.make_async_remote_copy(
+            src_ref=wbuf[s].at[pl.ds(start, size)],
+            dst_ref=wbuf[s].at[pl.ds(half + start, size)],
+            send_sem=fw_send.at[s, k],
+            recv_sem=fw_recv.at[s, k],
+            device_id=partner(1),
             device_id_type=MESH,
         )
 
@@ -119,32 +141,61 @@
         for s in range(streams):
             if k:
                 ag_copy(s, k - 1).wait_recv()
-            if k < bits:
+            if k < bits - 1:
                 ag_copy(s, k).start()
-
-    def rs_copy(s, k):
+            forward(s, k).start()
+
+    def pair_copy(q):
         return pltpu.make_async_remote_copy(
-            src_ref=send[s][k],
-            dst_ref=recv[s][k],
-            send_sem=rs_send.at[s, k],
-            recv_sem=rs_recv.at[s, k],
-            device_id=partner(orders[s][k]),
+            src_ref=sent.at[q],
+            dst_ref=came.at[q],
+            send_sem=pair_send.at[q],
+            recv_sem=pair_recv.at[q],
+            device_id=partner(1),
             device_id_type=MESH,
         )
 
+    def rs_copy(s, k, c):
+        size = count >> (k + 1)
+        low = size // 2
+        span = pl.ds(0, 1) if size == 1 else pl.ds(low * c, low)
+        return pltpu.make_async_remote_copy(
+            src_ref=send[s][k].at[span],
+            dst_ref=recv[s][k].at[span],
+            send_sem=rs_send.at[s, k, c],
+            recv_sem=rs_recv.at[s, k, c],
+            device_id=partner(1 << orders[s][k]),
+            device_id_type=MESH,
+        )
+
+    def halves(k):
+        return (1, 0) if count >> (k + 1) > 1 else (0,)
+
+    def incoming(s, k, p):
+        if k:
+            return recv[s][k][p].astype(F32)
+        return came[at_place(s, p) // 2, goff[s]: goff[s] + gsize[s], :].astype(F32)
+
     def rs_step(k):
-        half = count >> (k + 1)
-        low = half // 2
+        low = count >> (k + 2)
+        if k == 0:
+            for q in range(half):
+                pair_copy(q).wait_recv()
         for s in range(streams):
-            rs_copy(s, k).wait_recv()
+            if k:
+                rs_copy(s, k, 1).wait_recv()
+            for c in halves(k + 1):
+                size = max(1, low // 2)
+                for p in range(c * size, (c + 1) * size):
+                    send[s][k + 1][p] = (
+                        acc[s][low + p] + incoming(s, k, low + p)
+                    ).astype(BF16)
+                rs_copy(s, k + 1, c).start()
+        for s in range(streams):
+            if k:
+                rs_copy(s, k, 0).wait_recv()
             for p in range(low):
-                send[s][k + 1][p] = (
-                    acc[s][low + p] + recv[s][k][low + p].astype(F32)
-                ).astype(BF16)
-            rs_copy(s, k + 1).start()
-        for s in range(streams):
-            for p in range(low):
-                acc[s][p] = acc[s][p] + recv[s][k][p].astype(F32)
+                acc[s][p] = acc[s][p] + incoming(s, k, p)
 
     ag_step(0)
 
@@ -170,7 +221,7 @@
 
     cot_t = cot_ref[...].T
 
-    def weight_terms(flip):
+    def weight_terms(flip, begin, end):
         def body(q, carry):
             r = 2 * q + flip
             i = block_of(r)
@@ -178,24 +229,24 @@
             hidden = (normed * gain_of(i)).astype(BF16)
             hid[:, columns(i)] = hidden
             terms = jnp.dot(cot_t, hidden, preferred_element_type=F32)
-            for s in range(streams):
-                part = terms[goff[s]: goff[s] + gsize[s]]
-                if flip:
-                    send[s][0][place(s, r) - count // 2] = part.astype(BF16)
-                else:
-                    acc[s][place(s, r)] = part
+            if flip:
+                sent[q] = terms.astype(BF16)
+                pair_copy(q).start()
+            else:
+                for s in range(streams):
+                    acc[s][place(s, r)] = terms[goff[s]: goff[s] + gsize[s]]
             return carry
 
-        lax.fori_loop(0, count // 2, body, 0, unroll=4)
-
-    weight_terms(1)
-    for s in range(streams):
-        rs_copy(s, 0).start()
+        lax.fori_loop(begin, end, body, 0, unroll=4)
+
+    weight_terms(1, 0, quarter)
     ag_step(2)
-    weight_terms(0)
+    weight_terms(1, quarter, half)
+    weight_terms(0, 0, quarter)
+    for k in range(3, bits - 1):
+        ag_step(k)
+    weight_terms(0, quarter, half)
     rs_step(0)
-    for k in range(3, bits):
-        ag_step(k)
 
     def weight_pass(flip, begin, end, total):
         def body(q, total):
@@ -210,29 +261,49 @@
 
         return lax.fori_loop(begin, end, body, total, unroll=4)
 
-    half, quarter = count // 2, count // 4
     rs_step(1)
+    ag_step(bits - 1)
     total = weight_pass(0, 0, half, jnp.zeros((toks, heads), F32))
     rs_step(2)
-    ag_step(bits)
+    for s in range(streams):
+        for k in range(bits):
+            forward(s, k).wait_recv()
     total = weight_pass(1, 0, quarter, total)
     for k in range(3, bits - 1):
         rs_step(k)
     total = weight_pass(1, quarter, half, total)
 
-    def gain_copy(j):
-        return pltpu.make_async_remote_copy(
-            src_ref=gmine,
-            dst_ref=gall.at[me],
-            send_sem=g_send.at[j],
-            recv_sem=g_recv.at[j],
-            device_id=device((me + j) % count),
-            device_id_type=MESH,
-        )
+    sends, spans, ranks = [], [], [0]
+    for g in groups:
+        steps = [sum(1 << k for n, k in enumerate(g) if m >> n & 1) for m in range(1, 1 << len(g))]
+        spans.append([(r, len(ranks) * (m + 1), len(ranks)) for m, r in enumerate(steps)])
+        ranks = ranks + [x + r for r in steps for x in ranks]
+
+    def gain_copies(phase):
+        base = sum(len(span) for span in spans[:phase])
+        return [
+            pltpu.make_async_remote_copy(
+                src_ref=gall.at[pl.ds(0, size)],
+                dst_ref=gall.at[pl.ds(start, size)],
+                send_sem=g_send.at[base + n],
+                recv_sem=g_recv.at[base + n],
+                device_id=partner(r),
+                device_id_type=MESH,
+            )
+            for n, (r, start, size) in enumerate(spans[phase])
+        ]
+
+    def gain_step(phase):
+        if phase:
+            for copy in gain_copies(phase - 1):
+                copy.wait_recv()
+        if phase < len(groups):
+            for copy in gain_copies(phase):
+                copy.start()
 
     pieces = []
     for s in range(streams):
-        rs_copy(s, bits - 1).wait_recv()
+        rs_copy(s, bits - 1, 0).wait_recv()
         pieces.append((acc[s][0] + recv[s][bits - 1][0].astype(F32)) * scale)
     grad = jnp.concatenate(pieces, axis=0).T
     product = grad * w_ref[...].astype(F32)
@@ -241,14 +312,9 @@
         precision=lax.Precision.HIGHEST, preferred_element_type=F32,
     )
     own = sums[:1] / gain_of(me)
-    gmine[...] = own
-    gall[me] = own
-
-    def give(j, carry):
-        gain_copy(j).start()
-        return carry
-
-    lax.fori_loop(1, count, give, 0)
+    gall[0] = own
+    gain_step(0)
+
     wg_ref[...] = grad
     keys_ref[...] = total.astype(BF16)
     outs = [
@@ -277,35 +343,56 @@
             )
         )
         outs[-1].start()
-
-    def taken(j, carry):
-        gain_copy(j).wait_recv()
-        gain_copy(j).wait_send()
-        return carry
-
-    lax.fori_loop(1, count, taken, 0)
-    for b in range(count):
+        if g % 2 and g < 2 * len(groups) - 2:
+            gain_step(g // 2 + 1)
+    for phase in range(chunks // 2 + 1, len(groups) + 1):
+        gain_step(phase)
+    for p, r in enumerate(ranks):
+        i = block_of(r)
         for j in range(parts):
-            gg_ref[b * parts + j: b * parts + j + 1, :] = gall[b, :, j * 128: (j + 1) * 128]
+            gg_ref[pl.ds(i * parts + j, 1), :] = gall[p, :, j * 128: (j + 1) * 128]
     outs.append(pltpu.make_async_copy(gg_ref, gg_hbm, out_sem.at[2]))
     outs[-1].start()
     for s in range(streams):
         for k in range(bits):
-            ag_copy(s, k).wait_send()
-            rs_copy(s, k).wait_send()
+            forward(s, k).wait_send()
+            if k < bits - 1:
+                ag_copy(s, k).wait_send()
+            if k:
+                for c in halves(k):
+                    rs_copy(s, k, c).wait_send()
+    for q in range(half):
+        pair_copy(q).wait_send()
+    for phase in range(len(groups)):
+        for copy in gain_copies(phase):
+            copy.wait_send()
     for copy in outs:
         copy.wait()
 
 
-def hand_out(*refs):
-    sems = refs[-1]
-    pairs = (len(refs) - 1) // 2
-    copies = [
-        pltpu.make_async_copy(refs[n], refs[pairs + n], sems.at[n]) for n in range(pairs)
+def hand_out(pieces, *refs):
+    pairs = len(pieces)
+    here, there, between, into, out = (
+        refs[:pairs], refs[pairs: 2 * pairs], refs[2 * pairs: 3 * pairs], refs[-2], refs[-1]
+    )
+    cuts = []
+    for n, parts in enumerate(pieces):
+        rows = here[n].shape[0] // parts
+        cuts += [(n, pl.ds(m * rows, rows)) for m in range(parts)]
+    first = [
+        pltpu.make_async_copy(here[n].at[cut], between[n].at[cut], into.at[c])
+        for c, (n, cut) in enumerate(cuts)
     ]
-    for copy in copies:
+    second = [
+        pltpu.make_async_copy(between[n].at[cut], there[n].at[cut], out.at[c])
+        for c, (n, cut) in enumerate(cuts)
+    ]
+    for copy in first:
         copy.start()
-    for copy in copies:
+    for before, after in zip(first, second):
+        before.wait()
+        after.start()
+    for copy in second:
         copy.wait()
 
 
@@ -320,8 +407,9 @@
     stages = [
         pltpu.VMEM((count >> (k + 1), n * heads // 8, rows), BF16)
         for n in shares
-        for k in range(bits)
+        for k in range(1, bits)
     ]
+    pieces = [1, 8, 1, 1]
     shapes = (
         jax.ShapeDtypeStruct((toks, heads), BF16),
         jax.ShapeDtypeStruct((toks, width), BF16),
@@ -344,13 +432,13 @@
             pltpu.VMEM((width // 128, 128), F32),
             pltpu.VMEM((toks, 128), F32),
             pltpu.VMEM((toks, 128), F32),
-            pltpu.VMEM((1, rows), F32),
             pltpu.VMEM((count, 1, rows), F32),
         ]
         + [pltpu.VMEM((count, n * rows // 8, heads), BF16) for n in shares]
         + [pltpu.VMEM((count // 2, n * heads // 8, rows), F32) for n in shares]
         + stages
         + stages
+        + [pltpu.VMEM((count // 2, heads, rows), BF16)] * 2
         + [
             pltpu.SemaphoreType.DMA((4,)),
             pltpu.SemaphoreType.DMA((3,)),
@@ -359,8 +447,12 @@
             pltpu.SemaphoreType.DMA((len(shares), bits)),
             pltpu.SemaphoreType.DMA((len(shares), bits)),
             pltpu.SemaphoreType.DMA((len(shares), bits)),
-            pltpu.SemaphoreType.DMA((count,)),
-            pltpu.SemaphoreType.DMA((count,)),
+            pltpu.SemaphoreType.DMA((count // 2,)),
+            pltpu.SemaphoreType.DMA((count // 2,)),
+            pltpu.SemaphoreType.DMA((len(shares), bits, 2)),
+            pltpu.SemaphoreType.DMA((len(shares), bits, 2)),
+            pltpu.SemaphoreType.DMA((3 * bits,)),
+            pltpu.SemaphoreType.DMA((3 * bits,)),
         ],
         compiler_params=pltpu.CompilerParams(
             collective_id=0, has_side_effects=True, vmem_limit_bytes=58 * 2**20
@@ -370,11 +462,12 @@
         ),
     )(tokens, norm_gain.reshape(width // 128, 128), key_weight, key_cotangent)
     keys, tg, wg, gg = pl.pallas_call(
-        hand_out,
+        functools.partial(hand_out, pieces),
         out_shape=shapes,
         in_specs=[anywhere] * 4,
         out_specs=[hbm] * 4,
-        scratch_shapes=[pltpu.SemaphoreType.DMA((4,))],
+        scratch_shapes=[pltpu.VMEM(shape.shape, shape.dtype) for shape in shapes]
+        + [pltpu.SemaphoreType.DMA((sum(pieces),))] * 2,
         compiler_params=pltpu.CompilerParams(vmem_limit_bytes=58 * 2**20),
         cost_estimate=pl.CostEstimate(
             flops=0, bytes_accessed=4 * toks * width, transcendentals=0

time: 115 us -> 48.2 us (0.42)
  Pallas kernels: 114 us -> 46.8 us
    pallas_call x1, Pallas kernels: 70.6 us -> 2.51 us  [fused(): pl.pallas_call(functools.partial(hand_out, pieces), out_shape=shapes, in_...]
    pallas_call x1, Pallas kernels: 43.2 us -> 44.3 us  [fused(): pl.pallas_call(functools.partial(kernel, plan, local_count, scale), out_s...]
where the time goes in v3:
time: 48.2 us; the launch traced here: 47.5 us
  Pallas kernels  46.8 us (97%)
  between operations  0.64 us (1%)
    pallas_call x1, Pallas kernels, fused(): pl.pallas_call(functools.partial(kernel, plan, local_count, scale), out_s...  44.3 us
    pallas_call x1, Pallas kernels, fused(): pl.pallas_call(functools.partial(hand_out, pieces), out_shape=shapes, in_...  2.51 us

profile of v3, /device:TPU:0, one launch (start us, length us, event | category | flops | bytes accessed | tf_op | source)
XLA Modules:
  0.0 47.5 jit_solution(9877175218171487990)
XLA Ops:
  0.6 44.3 %shard_map.75 = (bf16[128,128]{1,0:T(8,128)(2,1)}, bf16[128,8192]{1,0:T(8,128)(2,1)}, f32[256,128]{1,0:T(8,128)}, f32[64,128]{1,0:T(8,128)}) custom-call(bf16[128,8192]{1,0:T(8,128)(2,1)} %tok_hbm.1, bf16[64,128]{1,0:T(8,128)(2,1)} %bitcast.3, bf16[256,128]{1,0:T(8,128)(2,1)} %w_hbm.1, bf16[128,128]{1,0:T(8,128)(2,1)} %cot_hbm.1), custom_call_target="tpu_custom_call" | custom-call | flops 805306368 | bytes 4194304 | tf_op jit(solution)/shard_map/pallas_call | solution.py:419
  45.0 2.5 %shard_map.76 = (bf16[128,128]{1,0:T(8,128)(2,1)}, bf16[128,8192]{1,0:T(8,128)(2,1)}, f32[256,128]{1,0:T(8,128)}, f32[64,128]{1,0:T(8,128)}) custom-call(bf16[128,128]{1,0:T(8,128)(2,1)} %get-tuple-element.12.refs_0_, bf16[128,8192]{1,0:T(8,128)(2,1)} %get-tuple-element.13.refs_1_, f32[256,128]{1,0:T(8,128)} %get-tuple-element.14.refs_2_, ...), custom_call_target="tpu_custom_call" | custom-call | bytes 4194304 | tf_op jit(solution)/shard_map/pallas_call | solution.py:464

commit v4 on v3

--- a/solution.py
+++ b/solution.py
@@ -52,7 +52,7 @@
     ) = list(it)
 
     me = lax.axis_index("node") * local_count + lax.axis_index("local")
-    mine = [(me // (1 << k)) % 2 for k in range(bits)]
+    flips = [(1 << k) * (1 - 2 * ((me // (1 << k)) % 2)) for k in range(bits)]
 
     def device(index):
         return (index // local_count, index % local_count)
@@ -61,16 +61,14 @@
         return device(block_of(r))
 
     def block_of(r):
-        total = 0
+        total = me
         for k in range(bits):
-            total = total + (1 << k) * ((mine[k] + r // (1 << k)) % 2)
+            if r >> k & 1:
+                total = total + flips[k]
         return total
 
     def place(s, r):
-        total = 0
-        for j, k in enumerate(orders[s]):
-            total = total + (1 << (bits - 1 - j)) * ((r // (1 << k)) % 2)
-        return total
+        return sum((r >> k & 1) << (bits - 1 - j) for j, k in enumerate(orders[s]))
 
     def at_place(s, p):
         return sum(((p >> (bits - 1 - j)) & 1) << k for j, k in enumerate(orders[s]))
@@ -222,7 +220,7 @@
     cot_t = cot_ref[...].T
 
     def weight_terms(flip, begin, end):
-        def body(q, carry):
+        for q in range(begin, end):
             r = 2 * q + flip
             i = block_of(r)
             normed = tok[:, columns(i)].astype(F32) * across(rstds)
@@ -235,9 +233,6 @@
             else:
                 for s in range(streams):
                     acc[s][place(s, r)] = terms[goff[s]: goff[s] + gsize[s]]
-            return carry
-
-        lax.fori_loop(begin, end, body, 0, unroll=4)
 
     weight_terms(1, 0, quarter)
     ag_step(2)
@@ -249,7 +244,7 @@
     rs_step(0)
 
     def weight_pass(flip, begin, end, total):
-        def body(q, total):
+        for q in range(begin, end):
             r = 2 * q + flip
             i = block_of(r)
             block = jnp.concatenate([wbuf[s][place(s, r)] for s in range(streams)], axis=0)
@@ -257,9 +252,8 @@
                 cot_ref[...], block, (((1,), (1,)), ((), ())), preferred_element_type=F32
             )
             back[:, columns(i)] = dhidden * gain_of(i) * across(rstds)
-            return total + jnp.dot(hid[:, columns(i)], block, preferred_element_type=F32)
-
-        return lax.fori_loop(begin, end, body, total, unroll=4)
+            total = total + jnp.dot(hid[:, columns(i)], block, preferred_element_type=F32)
+        return total
 
     rs_step(1)
     ag_step(bits - 1)

time: 48.2 us -> 48 us (level)
  no operation moved by 1% of the time
where the time goes in v4:
time: 48 us; the launch traced here: 47.3 us
  Pallas kernels  46.7 us (97%)
  between operations  0.64 us (1%)
    pallas_call x1, Pallas kernels, fused(): pl.pallas_call(functools.partial(kernel, plan, local_count, scale), out_s...  44.2 us
    pallas_call x1, Pallas kernels, fused(): pl.pallas_call(functools.partial(hand_out, pieces), out_shape=shapes, in_...  2.51 us

profile of v4, /device:TPU:0, one launch (start us, length us, event | category | flops | bytes accessed | tf_op | source)
XLA Modules:
  0.0 47.3 jit_solution(5268406735521620108)
XLA Ops:
  0.6 44.2 %shard_map.75 = (bf16[128,128]{1,0:T(8,128)(2,1)}, bf16[128,8192]{1,0:T(8,128)(2,1)}, f32[256,128]{1,0:T(8,128)}, f32[64,128]{1,0:T(8,128)}) custom-call(bf16[128,8192]{1,0:T(8,128)(2,1)} %tok_hbm.1, bf16[64,128]{1,0:T(8,128)(2,1)} %bitcast.3, bf16[256,128]{1,0:T(8,128)(2,1)} %w_hbm.1, bf16[128,128]{1,0:T(8,128)(2,1)} %cot_hbm.1), custom_call_target="tpu_custom_call" | custom-call | flops 805306368 | bytes 4194304 | tf_op jit(solution)/shard_map/pallas_call | solution.py:413
  44.8 2.5 %shard_map.76 = (bf16[128,128]{1,0:T(8,128)(2,1)}, bf16[128,8192]{1,0:T(8,128)(2,1)}, f32[256,128]{1,0:T(8,128)}, f32[64,128]{1,0:T(8,128)}) custom-call(bf16[128,128]{1,0:T(8,128)(2,1)} %get-tuple-element.12.refs_0_, bf16[128,8192]{1,0:T(8,128)(2,1)} %get-tuple-element.13.refs_1_, f32[256,128]{1,0:T(8,128)} %get-tuple-element.14.refs_2_, ...), custom_call_target="tpu_custom_call" | custom-call | bytes 4194304 | tf_op jit(solution)/shard_map/pallas_call | solution.py:458

commit v5 on v4

--- a/solution.py
+++ b/solution.py
@@ -16,13 +16,18 @@
 def stream_plan(bits):
     rest = list(range(1, bits))
     if bits == 5:
-        return [3, 3, 2], [[0, 1, 2, 3, 4], [0, 2, 3, 4, 1], [0, 3, 4, 1, 2]]
+        return [3, 3, 2], [[0, 1, 2, 3, 4], [0, 2, 1, 3, 4], [0, 3, 4, 1, 2]]
     return [4, 4], [[0] + rest, [0] + rest[::-1]]
 
 
 def gain_groups(bits):
-    rest = list(range(1, bits))
-    return [rest[max(0, n - 2): n] for n in range(len(rest), 0, -2)] + [[0]]
+    return [list(range(1, bits)), [0]]
+
+
+def masks(group):
+    return [
+        sum(1 << k for n, k in enumerate(group) if m >> n & 1) for m in range(1, 1 << len(group))
+    ]
 
 
 def kernel(
@@ -102,8 +107,8 @@
 
     barrier = pltpu.get_barrier_semaphore()
 
-    groups = [high for high in gain_groups(bits)]
-    friends = sorted({1 << k for k in range(bits)} | {sum(1 << k for k in g) for g in groups})
+    groups = gain_groups(bits)
+    friends = sorted({r for g in groups for r in masks(g)})
     for r in friends:
         pl.semaphore_signal(barrier, inc=1, device_id=partner(r), device_id_type=MESH)
     w_copy.wait()
@@ -269,7 +274,7 @@
 
     sends, spans, ranks = [], [], [0]
     for g in groups:
-        steps = [sum(1 << k for n, k in enumerate(g) if m >> n & 1) for m in range(1, 1 << len(g))]
+        steps = masks(g)
         spans.append([(r, len(ranks) * (m + 1), len(ranks)) for m, r in enumerate(steps)])
         ranks = ranks + [x + r for r in steps for x in ranks]
 
@@ -337,9 +342,9 @@
             )
         )
         outs[-1].start()
-        if g % 2 and g < 2 * len(groups) - 2:
-            gain_step(g // 2 + 1)
-    for phase in range(chunks // 2 + 1, len(groups) + 1):
+        if g == chunks // 2:
+            gain_step(1)
+    for phase in range(2, len(groups) + 1):
         gain_step(phase)
     for p, r in enumerate(ranks):
         i = block_of(r)
@@ -445,8 +450,8 @@
             pltpu.SemaphoreType.DMA((count // 2,)),
             pltpu.SemaphoreType.DMA((len(shares), bits, 2)),
             pltpu.SemaphoreType.DMA((len(shares), bits, 2)),
-            pltpu.SemaphoreType.DMA((3 * bits,)),
-            pltpu.SemaphoreType.DMA((3 * bits,)),
+            pltpu.SemaphoreType.DMA((count // 2,)),
+            pltpu.SemaphoreType.DMA((count // 2,)),
         ],
         compiler_params=pltpu.CompilerParams(
             collective_id=0, has_side_effects=True, vmem_limit_bytes=58 * 2**20

time: 48 us -> 46.1 us (0.960)
  Pallas kernels: 46.7 us -> 45 us
    pallas_call x1, Pallas kernels: 44.2 us -> 42.5 us  [fused(): pl.pallas_call(functools.partial(kernel, plan, local_count, scale), out_s...]
where the time goes in v5:
time: 46.1 us; the launch traced here: 45.6 us
  Pallas kernels  45 us (98%)
  between operations  0.64 us (1%)
    pallas_call x1, Pallas kernels, fused(): pl.pallas_call(functools.partial(kernel, plan, local_count, scale), out_s...  42.5 us
    pallas_call x1, Pallas kernels, fused(): pl.pallas_call(functools.partial(hand_out, pieces), out_shape=shapes, in_...  2.51 us

profile of v5, /device:TPU:0, one launch (start us, length us, event | category | flops | bytes accessed | tf_op | source)
XLA Modules:
  0.0 45.6 jit_solution(10439747313445577293)
XLA Ops:
  0.6 42.5 %shard_map.75 = (bf16[128,128]{1,0:T(8,128)(2,1)}, bf16[128,8192]{1,0:T(8,128)(2,1)}, f32[256,128]{1,0:T(8,128)}, f32[64,128]{1,0:T(8,128)}) custom-call(bf16[128,8192]{1,0:T(8,128)(2,1)} %tok_hbm.1, bf16[64,128]{1,0:T(8,128)(2,1)} %bitcast.3, bf16[256,128]{1,0:T(8,128)(2,1)} %w_hbm.1, bf16[128,128]{1,0:T(8,128)(2,1)} %cot_hbm.1), custom_call_target="tpu_custom_call" | custom-call | flops 805306368 | bytes 4194304 | tf_op jit(solution)/shard_map/pallas_call | solution.py:418
  43.1 2.5 %shard_map.76 = (bf16[128,128]{1,0:T(8,128)(2,1)}, bf16[128,8192]{1,0:T(8,128)(2,1)}, f32[256,128]{1,0:T(8,128)}, f32[64,128]{1,0:T(8,128)}) custom-call(bf16[128,128]{1,0:T(8,128)(2,1)} %get-tuple-element.12.refs_0_, bf16[128,8192]{1,0:T(8,128)(2,1)} %get-tuple-element.13.refs_1_, f32[256,128]{1,0:T(8,128)} %get-tuple-element.14.refs_2_, ...), custom_call_target="tpu_custom_call" | custom-call | bytes 4194304 | tf_op jit(solution)/shard_map/pallas_call | solution.py:463

commit v6 on v5

--- a/solution.py
+++ b/solution.py
@@ -260,17 +260,44 @@
             total = total + jnp.dot(hid[:, columns(i)], block, preferred_element_type=F32)
         return total
 
-    rs_step(1)
     ag_step(bits - 1)
     total = weight_pass(0, 0, half, jnp.zeros((toks, heads), F32))
-    rs_step(2)
+    rs_step(1)
     for s in range(streams):
         for k in range(bits):
             forward(s, k).wait_recv()
     total = weight_pass(1, 0, quarter, total)
+    rs_step(2)
+    total = weight_pass(1, quarter, half, total)
     for k in range(3, bits - 1):
         rs_step(k)
-    total = weight_pass(1, quarter, half, total)
+
+    keys_ref[...] = total.astype(BF16)
+    outs = [pltpu.make_async_copy(keys_ref, keys_hbm, out_sem.at[1])]
+    outs[-1].start()
+    inner = jnp.sum(total * cot_ref[...].astype(F32), axis=1, keepdims=True) * (1.0 / width)
+    rowco[...] = rstds[...] * rstds[...] * inner
+
+    def token_part(i, carry):
+        tg_ref[:, columns(i)] = (
+            back[:, columns(i)] - tok[:, columns(i)].astype(F32) * across(rowco)
+        ).astype(BF16)
+        return carry
+
+    def token_grad(g):
+        lax.fori_loop(
+            g * count // chunks, (g + 1) * count // chunks, token_part, 0, unroll=2
+        )
+        outs.append(
+            pltpu.make_async_copy(
+                tg_ref.at[:, pl.ds(g * cw, cw)], tg_hbm.at[:, pl.ds(g * cw, cw)],
+                out_sem.at[3 + g],
+            )
+        )
+        outs[-1].start()
+
+    for g in range(chunks // 2):
+        token_grad(g)
 
     sends, spans, ranks = [], [], [0]
     for g in groups:
@@ -315,35 +342,11 @@
     gain_step(0)
 
     wg_ref[...] = grad
-    keys_ref[...] = total.astype(BF16)
-    outs = [
-        pltpu.make_async_copy(wg_ref, wg_hbm, out_sem.at[0]),
-        pltpu.make_async_copy(keys_ref, keys_hbm, out_sem.at[1]),
-    ]
-    for copy in outs:
-        copy.start()
-    inner = jnp.sum(total * cot_ref[...].astype(F32), axis=1, keepdims=True) * (1.0 / width)
-    rowco[...] = rstds[...] * rstds[...] * inner
-
-    def token_part(i, carry):
-        tg_ref[:, columns(i)] = (
-            back[:, columns(i)] - tok[:, columns(i)].astype(F32) * across(rowco)
-        ).astype(BF16)
-        return carry
-
-    for g in range(chunks):
-        lax.fori_loop(
-            g * count // chunks, (g + 1) * count // chunks, token_part, 0, unroll=2
-        )
-        outs.append(
-            pltpu.make_async_copy(
-                tg_ref.at[:, pl.ds(g * cw, cw)], tg_hbm.at[:, pl.ds(g * cw, cw)],
-                out_sem.at[3 + g],
-            )
-        )
-        outs[-1].start()
-        if g == chunks // 2:
-            gain_step(1)
+    outs.append(pltpu.make_async_copy(wg_ref, wg_hbm, out_sem.at[0]))
+    outs[-1].start()
+    for g in range(chunks // 2, chunks):
+        token_grad(g)
+    gain_step(1)
     for phase in range(2, len(groups) + 1):
         gain_step(phase)
     for p, r in enumerate(ranks):

time: 46.1 us -> 45.8 us (level)
  Pallas kernels: 45 us -> 44.5 us
    pallas_call x1, Pallas kernels: 42.5 us -> 42 us  [fused(): pl.pallas_call(functools.partial(kernel, plan, local_count, scale), out_s...]
where the time goes in v6:
time: 45.8 us; the launch traced here: 45.1 us
  Pallas kernels  44.5 us (97%)
  between operations  0.64 us (1%)
    pallas_call x1, Pallas kernels, fused(): pl.pallas_call(functools.partial(kernel, plan, local_count, scale), out_s...  42 us
    pallas_call x1, Pallas kernels, fused(): pl.pallas_call(functools.partial(hand_out, pieces), out_shape=shapes, in_...  2.51 us

profile of v6, /device:TPU:0, one launch (start us, length us, event | category | flops | bytes accessed | tf_op | source)
XLA Modules:
  0.0 45.1 jit_solution(8216415492451112227)
XLA Ops:
  0.6 42.0 %shard_map.75 = (bf16[128,128]{1,0:T(8,128)(2,1)}, bf16[128,8192]{1,0:T(8,128)(2,1)}, f32[256,128]{1,0:T(8,128)}, f32[64,128]{1,0:T(8,128)}) custom-call(bf16[128,8192]{1,0:T(8,128)(2,1)} %tok_hbm.1, bf16[64,128]{1,0:T(8,128)(2,1)} %bitcast.3, bf16[256,128]{1,0:T(8,128)(2,1)} %w_hbm.1, bf16[128,128]{1,0:T(8,128)(2,1)} %cot_hbm.1), custom_call_target="tpu_custom_call" | custom-call | flops 805306368 | bytes 4194304 | tf_op jit(solution)/shard_map/pallas_call | solution.py:421
  42.6 2.5 %shard_map.76 = (bf16[128,128]{1,0:T(8,128)(2,1)}, bf16[128,8192]{1,0:T(8,128)(2,1)}, f32[256,128]{1,0:T(8,128)}, f32[64,128]{1,0:T(8,128)}) custom-call(bf16[128,128]{1,0:T(8,128)(2,1)} %get-tuple-element.12.refs_0_, bf16[128,8192]{1,0:T(8,128)(2,1)} %get-tuple-element.13.refs_1_, f32[256,128]{1,0:T(8,128)} %get-tuple-element.14.refs_2_, ...), custom_call_target="tpu_custom_call" | custom-call | bytes 4194304 | tf_op jit(solution)/shard_map/pallas_call | solution.py:466

commit v7 on v6

--- a/solution.py
+++ b/solution.py
@@ -204,6 +204,8 @@
 
     squares = jnp.zeros((toks, 128), F32)
     for c in range(chunks):
+        if c == chunks // 2:
+            ag_step(1)
         tok_copies[c].wait()
 
         def square(j, total, c=c):
@@ -219,8 +221,6 @@
     gain_copy_in.wait()
     gains[...] = gain_ref[...].astype(F32)
     cot_copy.wait()
-
-    ag_step(1)
 
     cot_t = cot_ref[...].T
 

time: 45.8 us -> 45.9 us (level)
  no operation moved by 1% of the time
where the time goes in v7:
time: 45.9 us; the launch traced here: 45.3 us
  Pallas kernels  44.6 us (97%)
  between operations  0.64 us (1%)
    pallas_call x1, Pallas kernels, fused(): pl.pallas_call(functools.partial(kernel, plan, local_count, scale), out_s...  42.1 us
    pallas_call x1, Pallas kernels, fused(): pl.pallas_call(functools.partial(hand_out, pieces), out_shape=shapes, in_...  2.51 us

profile of v7, /device:TPU:0, one launch (start us, length us, event | category | flops | bytes accessed | tf_op | source)
XLA Modules:
  0.0 45.3 jit_solution(7487866988361155992)
XLA Ops:
  0.6 42.1 %shard_map.75 = (bf16[128,128]{1,0:T(8,128)(2,1)}, bf16[128,8192]{1,0:T(8,128)(2,1)}, f32[256,128]{1,0:T(8,128)}, f32[64,128]{1,0:T(8,128)}) custom-call(bf16[128,8192]{1,0:T(8,128)(2,1)} %tok_hbm.1, bf16[64,128]{1,0:T(8,128)(2,1)} %bitcast.3, bf16[256,128]{1,0:T(8,128)(2,1)} %w_hbm.1, bf16[128,128]{1,0:T(8,128)(2,1)} %cot_hbm.1), custom_call_target="tpu_custom_call" | custom-call | flops 805306368 | bytes 4194304 | tf_op jit(solution)/shard_map/pallas_call | solution.py:421
  42.7 2.5 %shard_map.76 = (bf16[128,128]{1,0:T(8,128)(2,1)}, bf16[128,8192]{1,0:T(8,128)(2,1)}, f32[256,128]{1,0:T(8,128)}, f32[64,128]{1,0:T(8,128)}) custom-call(bf16[128,128]{1,0:T(8,128)(2,1)} %get-tuple-element.12.refs_0_, bf16[128,8192]{1,0:T(8,128)(2,1)} %get-tuple-element.13.refs_1_, f32[256,128]{1,0:T(8,128)} %get-tuple-element.14.refs_2_, ...), custom_call_target="tpu_custom_call" | custom-call | bytes 4194304 | tf_op jit(solution)/shard_map/pallas_call | solution.py:466
